TPU v7x, 768 devices: a whole 4x8x12 slice. The times are simulated.
768 devices in a mesh: phase: 3 (over z_hi), dp: 8 (over y), mp: 32 (over x, z_lo, core).
Axes of the slice: x: 4, y: 8, z: 12 (z_hi: 3, z_lo: 4; z = z_hi * 4 + z_lo), core: 2. Of those that a mesh axis runs over, the one named last changes fastest.
Arguments:
- memory: bfloat16 [8, 256, 1024], P('dp', None, 'mp'), may hold values from -6 to 6
- states: bfloat16 [3, 8, 256, 1024], P('phase', 'dp', None, 'mp'), may hold values from -6 to 6
- targets: bfloat16 [3, 8, 256, 1024], P('phase', 'dp', None, 'mp'), may hold values from -6 to 6
- w_query: bfloat16 [3, 1024, 16384], P('phase', None, 'mp'), may hold values from -0.1875 to 0.1875
- w_key: bfloat16 [3, 1024, 16384], P('phase', None, 'mp'), may hold values from -0.1875 to 0.1875
- w_value: bfloat16 [3, 1024, 16384], P('phase', None, 'mp'), may hold values from -0.1875 to 0.1875
- w_out: bfloat16 [3, 16384, 1024], P('phase', 'mp'), may hold values from -0.046875 to 0.046875
- src_ids: int32 [8, 256], P('dp'), may hold values from 0 to 3, never falling along the last dimension, each value on 1 to 128 neighbouring positions
- tgt_ids: int32 [8, 256], P('dp'), may hold values from 0 to 3, never falling along the last dimension, each value on 1 to 128 neighbouring positions
- counts: int32 [8], P('dp'), may hold values from 1 to 256
Outputs:
- cross_out: bfloat16 [3, 8, 256, 1024], P('phase', 'dp', None, 'mp')
- loss: float32 [3], P('phase')
- states_grad: bfloat16 [3, 8, 256, 1024], P('phase', 'dp', None, 'mp')
- memory_grad: bfloat16 [8, 256, 1024], P('dp', None, 'mp')
Inputs may be any that keep to these rules, and one draw needn't show every extreme that they name: `src_ids`: both id arrays of a sample hold all segment numbers 0 to 3.
All inputs are finite; a program needn't handle non-finite values.
Results may differ from a plain program's by a relative error of at most 0.013.
The roundings to bfloat16 on the way count: a program that leaves them out, or rounds other values in their place, can miss the bound.
Values may be sent and summed in bfloat16 or wider, within the bound.
A program may use at most 32 MiB of HBM per device.

v0:
```python
import jax
import jax.numpy as jnp
from jax import lax
from jax.sharding import PartitionSpec as P

HEAD = 128


def local(memory, states, targets, w_query, w_key, w_value, w_out, src_ids, tgt_ids, counts):
    count_local = jnp.sum(counts.astype(jnp.float32))
    total = lax.psum(count_local, "dp")
    mem_all, state_all, target_all = (
        lax.all_gather(memory, "mp", axis=2, tiled=True),
        lax.all_gather(states[0], "mp", axis=2, tiled=True),
        lax.all_gather(targets[0], "mp", axis=2, tiled=True),
    )
    wq = w_query[0]
    wk = w_key[0]
    wv = w_value[0]
    wo = w_out[0]
    batch = mem_all.shape[0]
    src_len = mem_all.shape[1]
    tgt_len = state_all.shape[1]
    local_inner = wq.shape[1]
    local_heads = local_inner // HEAD
    query = jnp.einsum("btd,dk->btk", state_all, wq, preferred_element_type=jnp.float32).astype(
        jnp.bfloat16
    )
    keys = jnp.einsum("bjd,dk->bjk", mem_all, wk, preferred_element_type=jnp.float32).astype(
        jnp.bfloat16
    )
    values = jnp.einsum("bjd,dk->bjk", mem_all, wv, preferred_element_type=jnp.float32).astype(
        jnp.bfloat16
    )
    query_h = query.reshape(batch, tgt_len, local_heads, HEAD)
    keys_h = keys.reshape(batch, src_len, local_heads, HEAD)
    values_h = values.reshape(batch, src_len, local_heads, HEAD)
    scores = jnp.einsum("bthe,bjhe->bhtj", query_h, keys_h, preferred_element_type=jnp.float32)
    allowed = tgt_ids[:, None, :, None] == src_ids[:, None, None, :]
    scores = jnp.where(allowed, scores, -1e30)
    probs = jax.nn.softmax(scores, axis=-1)
    probs_low = probs.astype(jnp.bfloat16)
    attended = jnp.einsum(
        "bhtj,bjhe->bthe", probs_low, values_h, preferred_element_type=jnp.float32
    )
    attended = attended.astype(jnp.bfloat16).reshape(batch, tgt_len, local_inner)
    out_part = jnp.einsum("btk,kd->btd", attended, wo, preferred_element_type=jnp.float32)
    valid = (jnp.arange(tgt_len)[None, :] < counts[:, None]).astype(jnp.bfloat16)
    grad_out = target_all * valid[:, :, None]
    grad_att = jnp.einsum("btd,kd->btk", grad_out, wo, preferred_element_type=jnp.float32)
    grad_att = grad_att.astype(jnp.bfloat16).reshape(batch, tgt_len, local_heads, HEAD)
    grad_prob = jnp.einsum(
        "bthe,bjhe->bhtj", grad_att, values_h, preferred_element_type=jnp.float32
    )
    inner = jnp.sum(probs * grad_prob, axis=-1, keepdims=True)
    grad_score = (probs * (grad_prob - inner)).astype(jnp.bfloat16)
    grad_q = jnp.einsum("bhtj,bjhe->bthe", grad_score, keys_h, preferred_element_type=jnp.float32)
    grad_q = grad_q.astype(jnp.bfloat16).reshape(batch, tgt_len, local_inner)
    grad_k = jnp.einsum("bhtj,bthe->bjhe", grad_score, query_h, preferred_element_type=jnp.float32)
    grad_k = grad_k.astype(jnp.bfloat16).reshape(batch, src_len, local_inner)
    grad_v = jnp.einsum("bhtj,bthe->bjhe", probs_low, grad_att, preferred_element_type=jnp.float32)
    grad_v = grad_v.astype(jnp.bfloat16).reshape(batch, src_len, local_inner)
    grad_x_part = jnp.einsum("btk,dk->btd", grad_q, wq, preferred_element_type=jnp.float32)
    grad_m_part = jnp.einsum("bjk,dk->bjd", grad_k, wk, preferred_element_type=jnp.float32)
    grad_m_part = grad_m_part + jnp.einsum(
        "bjk,dk->bjd", grad_v, wv, preferred_element_type=jnp.float32
    )
    out_sum = lax.psum_scatter(out_part, "mp", scatter_dimension=2, tiled=True)
    grad_x, grad_m = (
        lax.psum_scatter(grad_x_part, "mp", scatter_dimension=2, tiled=True),
        lax.psum_scatter(grad_m_part, "mp", scatter_dimension=2, tiled=True),
    )
    out_low = out_sum.astype(jnp.bfloat16)
    grad_local = targets[0] * valid[:, :, None]
    loss_part = jnp.sum(out_low.astype(jnp.float32) * grad_local.astype(jnp.float32))
    loss_total = lax.psum(loss_part, ("dp", "mp"))
    grad_mem = lax.psum(grad_m, "phase")
    loss = (loss_total / total).reshape(1)
    states_grad = (grad_x / total).astype(jnp.bfloat16)[None]
    memory_grad = (grad_mem / total).astype(jnp.bfloat16)
    return (out_low[None], loss, states_grad, memory_grad)


def solution(mesh):
    placed = (
        P("dp", None, "mp"),
        P("phase", "dp", None, "mp"),
        P("phase", "dp", None, "mp"),
        P("phase", None, "mp"),
        P("phase", None, "mp"),
        P("phase", None, "mp"),
        P("phase", "mp", None),
        P("dp", None),
        P("dp", None),
        P("dp"),
    )
    return jax.shard_map(
        local,
        mesh=mesh,
        in_specs=placed,
        out_specs=(
            P("phase", "dp", None, "mp"),
            P("phase"),
            P("phase", "dp", None, "mp"),
            P("dp", None, "mp"),
        ),
        check_vma=False,
    )
```

profile of v0, /device:TPU:8, one launch (start us, length us, event | category | flops | bytes accessed | tf_op | source)
XLA Modules:
  0.0 1115.5 jit_solution(56116839935737429)
XLA Ops:
  7.2 0.0 copy-start
  7.2 0.0 copy-start.15
  7.2 0.0 all-reduce.7.cloned.1.call-start
  7.2 51.0 %all_gather.9 = bf16[1,256,1024]{1,2,0:T(8,128)(2,1)} all-gather(bf16[1,256,32]{1,2,0:T(8,128)(2,1)} %param.10), channel_id=1, replica_groups=mesh['phase'=3,'dp'=8,'mp'=32] {'mp'}, dimensions={2}, use_global_device_ids=true | all-gather | bytes 540672 | tf_op jit(solution)/shard_map/all_gather | solution.py:13
  58.2 0.0 copy-done.15
  58.2 40.0 %all-gather = bf16[1,1,256,1024]{2,3,1,0:T(8,128)(2,1)S(1)} all-gather(bf16[1,1,256,32]{2,3,1,0:T(8,128)(2,1)S(1)} %copy-done.15), channel_id=2, replica_groups=mesh['phase'=3,'dp'=8,'mp'=32] {'mp'}, dimensions={3}, use_global_device_ids=true | all-gather | bytes 540672 | tf_op jit(solution)/shard_map/all_gather | solution.py:14
  98.3 0.0 copy-done
  98.3 0.0 copy-start.2
  98.3 0.5 convolution_convert_fusion.6
  98.7 0.1 copy.68
  98.9 0.6 copy-done.2
  99.5 0.0 copy-start.6
  99.5 0.0 copy-start.1
  99.5 2.3 fusion.4
  101.8 0.0 copy-done.1
  101.8 0.0 copy-done.11
  101.8 1.2 convolution_convert_fusion.5
  103.0 1.8 copy.69
  105.5 0.0 copy-done.14
  105.5 41.3 %all-gather.1 = bf16[1,1,256,1024]{2,3,1,0:T(8,128)(2,1)S(1)} all-gather(bf16[1,1,256,32]{2,3,1,0:T(8,128)(2,1)S(1)} %copy-done.14), channel_id=3, replica_groups=mesh['phase'=3,'dp'=8,'mp'=32] {'mp'}, dimensions={3}, use_global_device_ids=true | all-gather | bytes 540672 | tf_op jit(solution)/shard_map/all_gather | solution.py:15
  146.8 0.0 copy-done.4
  146.8 1.2 convolution_convert_fusion.3
  148.0 1.8 copy.70
  149.8 0.0 copy-done.17
  149.8 0.7 copy-done.16
  150.5 0.1 broadcast_compare_fusion
  150.6 1.5 fusion.31
  152.0 1.3 multiply_reduce_fusion
  153.4 0.0 copy-start.8
  153.4 0.2 multiply_convert_fusion
  153.6 0.8 copy-done.8
  154.3 0.9 convolution_convert_fusion.2
  155.2 0.3 convolution_convert_fusion.1
  155.6 0.0 copy-done.6
  155.6 0.6 copy-done.9
  156.2 0.1 copy-done.12
  156.3 1.5 convolution_convert_fusion
  157.8 1.4 convolution_bitcast_fusion
  159.2 1.9 copy.56
  161.1 0.5 fusion.7
  161.6 0.7 copy-done.3
  162.3 0.0 copy-done.13
  162.4 0.5 fusion.3
  162.8 1.9 copy.62
  164.8 0.0 all-reduce.7.cloned.1.call-update
  164.8 0.9 copy-done.7
  165.7 0.1 copy-done.10
  165.8 0.1 copy-done.18
  165.9 0.8 convolution_convert_fusion.4
  166.6 0.5 copy-done.5
  167.1 0.5 convolution_bitcast_fusion.1
  167.6 0.8 copy.50
  168.3 1.3 dynamic-slice
  170.3 218.0 %all-reduce.8 = bf16[1,256,1024]{1,0,2:T(2,128)(2,1)S(1)} all-reduce(f32[1,256,1024]{1,0,2:T(1,128)S(1)} %copy.50), channel_id=4, replica_groups=mesh['phase'=3,'dp'=8,'mp'=32] {'mp'}, use_global_device_ids=true, to_apply=%region_2.3.clone | all-reduce | flops 262144 | bytes 1572864
  388.4 0.6 multiply_reduce_fusion.1
  389.0 592.2 %psum.21 = f32[]{:T(128)} all-reduce(f32[]{:T(128)} %multiply_reduce_fusion.1), channel_id=1, replica_groups=mesh['phase'=3,'dp'=8,'mp'=32] {'dp','mp'}, use_global_device_ids=true, to_apply=%region_4.5 | all-reduce | flops 1 | bytes 8 | tf_op jit(solution)/shard_map/psum | solution.py:76
  981.1 94.7 %psum.22 = f32[]{:T(128)} all-reduce(f32[]{:T(128)} %bitcast.15), channel_id=1, replica_groups=mesh['phase'=3,'dp'=8,'mp'=32] {'dp'}, use_global_device_ids=true, to_apply=%region_5.6 | all-reduce | flops 1 | bytes 8 | tf_op jit(solution)/shard_map/psum | solution.py:11
  1075.8 0.6 copy.92
  1077.7 0.0 all-reduce.7.cloned.1.call-done
  1077.8 0.8 constant_dynamic-slice_fusion.1
  1078.5 1.2 fusion.27
  1079.8 0.8 constant_dynamic-slice_fusion
  1080.5 25.8 %psum.23 = f32[1,256,32]{1,2,0:T(8,128)S(1)} all-reduce(f32[1,256,32]{1,2,0:T(8,128)S(1)} %copy.63), channel_id=1, replica_groups=mesh['phase'=3,'dp'=8,'mp'=32] {'phase'}, use_global_device_ids=true, to_apply=%region_9.10 | all-reduce | flops 8192 | bytes 65536 | tf_op jit(solution)/shard_map/psum | solution.py:77
  1106.3 1.2 divide_convert_fusion
  (16 shorter events, 0.1 us)
Async XLA Ops:
  7.2 91.1 %copy-start = (bf16[1,1024,512]{2,1,0:T(8,128)(2,1)S(1)}, bf16[1,1024,512]{2,1,0:T(8,128)(2,1)}, u32[]{:S(2)}) copy-start(bf16[1,1024,512]{2,1,0:T(8,128)(2,1)} %param.13) | copy-start | bytes 3145732
  7.2 51.1 %copy-start.15 = (bf16[1,1,256,32]{2,3,1,0:T(8,128)(2,1)S(1)}, bf16[1,1,256,32]{2,3,1,0:T(8,128)(2,1)}, u32[]{:S(2)}) copy-start(bf16[1,1,256,32]{2,3,1,0:T(8,128)(2,1)} %param.11) | copy-start | bytes 49156
  7.2 1070.6 %all-reduce.7.cloned.1.call-start = ((), (), s32[]{:S(2)}) async-start(), calls=%async_computation | async-start | bytes 4194304
  98.3 1.2 copy-start.2
  99.5 56.1 %copy-start.6 = (bf16[256,512]{0,1:T(8,128)(2,1)}, bf16[256,512]{0,1:T(8,128)(2,1)S(1)}, u32[]{:S(2)}) copy-start(bf16[256,512]{0,1:T(8,128)(2,1)S(1)} %copy.68) | copy-start | bytes 786436
  99.5 2.3 copy-start.1
  99.5 2.3 copy-start.11
  101.8 44.9 %copy-start.4 = (bf16[1,512,1024]{2,1,0:T(8,128)(2,1)S(1)}, bf16[1,512,1024]{2,1,0:T(8,128)(2,1)}, u32[]{:S(2)}) copy-start(bf16[1,512,1024]{2,1,0:T(8,128)(2,1)} %param.16) | copy-start | bytes 3145732
  103.0 2.5 copy-start.14
  148.0 1.8 copy-start.17
  149.8 0.7 copy-start.16
  153.4 1.0 copy-start.8
  155.2 0.9 copy-start.9
  155.2 1.0 copy-start.12
  161.1 1.2 copy-start.3
  161.1 1.3 copy-start.13
  164.8 0.9 copy-start.7
  164.8 1.0 copy-start.10
  164.8 1.1 copy-start.18
  165.9 1.2 copy-start.5
Sparse Core Ops, SparseCore 0:
  164.9 305.7 all-reduce.6
where the time goes:
time: 1120 us
  blocking collectives  1060 us (95%)
  between operations  18 us (2%)
  local copies, waits for them, and re-layouts  16.9 us (2%)
  matrix products  14.2 us (1%)
    psum x1, blocking collectives, local(): loss_total = lax.psum(loss_part, ('dp', 'mp'))  592 us
    unnamed x1, blocking collectives  218 us
    psum x1, blocking collectives, local(): total = lax.psum(count_local, 'dp')  94.7 us
    all_gather x1, blocking collectives, local(): lax.all_gather(memory, 'mp', axis=2, tiled=True)  51 us
    all_gather x1, blocking collectives, local(): lax.all_gather(targets[0], 'mp', axis=2, tiled=True)  41.3 us
    all_gather x1, blocking collectives, local(): lax.all_gather(states[0], 'mp', axis=2, tiled=True)  40 us
    psum x1, blocking collectives, local(): grad_mem = lax.psum(grad_m, 'phase')  25.8 us
  transfers between devices with their start and end apart: 1, of which 0 were waited for; matrix products, arithmetic and copies ran while one was open for 0% of the time, Pallas kernels for 0%

commit v1 on v0

v1 whole, which is shorter than its diff:
```python
import jax
import jax.numpy as jnp
from jax import lax
from jax.experimental import pallas as pl
from jax.experimental.pallas import tpu as pltpu
from jax.sharding import PartitionSpec as P


BF = jnp.bfloat16
F32 = jnp.float32
MESH = pl.DeviceIdType.MESH
HEADS = 4
HEAD = 128
TOK = 256
NEG = -1e30
M, S, T = 0, 1, 2
OUT, GM, GX = 0, 1, 2


def nn(a, b):
    return lax.dot_general(a, b, (((1,), (0,)), ((), ())), preferred_element_type=F32)


def nt(a, b):
    return lax.dot_general(a, b, (((1,), (1,)), ((), ())), preferred_element_type=F32)


def main_kernel(
    mem_in, st_in, tg_in, wq_in, wk_in, wv_in, wo_in, src_ref, tgt_ref, cnt_ref,
    out_o, gx_o, gm_o, loss_o,
    wq, wk, wv, wo, wot, g, xt, bias,
    q_s, k_s, v_s, kt_s, vt_s, do_s, p_s, pb_s, ot_s, dqt_s, dk_s, dv_s,
    pb_out, po, lc, sx, lx, uo, ub, lz, lp, cs, l0, l1, l2, l3,
    lw, r_a, r_b, r_c, s_ab, s_c, rr_c, rr_x, rr_z, rs_c, rs_x, rs_z, r_p, s_p, r_k, s_k, r_l, s_l,
):
    p = lax.axis_index("phase")
    y = lax.axis_index("dp")
    m = lax.axis_index("mp")
    x, z, c = m // 8, (m // 2) % 4, m % 2
    ring_at = p * 4 + z

    sib = (p, y, x * 8 + z * 2 + (1 - c))

    def dev_x(d):
        return (p, y, ((x + d) % 4) * 8 + z * 2 + c)

    def dev_z(zz):
        return (p, y, x * 8 + zz * 2 + c)

    def dev_ring(d):
        at = (ring_at + d + 12) % 12
        return (at // 4, y, x * 8 + (at % 4) * 2 + c)

    def dev_y(d):
        return (p, (y + d) % 8, m)

    def zx(v):
        return (z, z + 1 - 2 * (z % 2), (z + 2) % 4, 3 - z)[v]

    def send(src, dst, ss, rs, dev):
        pltpu.make_async_remote_copy(
            src_ref=src, dst_ref=dst, send_sem=ss, recv_sem=rs, device_id=dev, device_id_type=MESH
        ).start()

    def wait(ref, sem):
        pltpu.make_async_copy(ref, ref, sem).wait()

    own = x * 4 + z
    loads = [pltpu.make_async_copy(src, g.at[a, c, own], lw.at[a]) for a, src in ((M, mem_in), (S, st_in), (T, tg_in))]
    loads.append(pltpu.make_async_copy(wo_in, wo, lw.at[3]))
    for i, (src, dst) in enumerate(((wk_in, wk), (wv_in, wv), (wq_in, wq))):
        for h in range(2):
            loads.append(pltpu.make_async_copy(src.at[:, h], dst.at[h], lw.at[4 + 2 * i + h]))
    for load in loads:
        load.start()

    barrier = pltpu.get_barrier_semaphore()
    greeted = [sib] + [dev_x(d) for d in (1, 2, 3)] + [dev_y(d) for d in range(1, 8)]
    greeted += [dev_ring(d) for d in (-4, -3, -2, -1, 1, 2, 3, 4)]
    for dev in greeted:
        pl.semaphore_signal(barrier, inc=1, device_id=dev, device_id_type=MESH)

    count = cnt_ref[0]
    src_col = jnp.transpose(jnp.broadcast_to(src_ref[...].astype(F32), (TOK, TOK)))
    bias[...] = jnp.where(src_col == tgt_ref[...].astype(F32), 0.0, NEG)
    cs[y] = jnp.full((8, 128), count.astype(F32))
    loads[3].wait()
    for b in range(8):
        part = jnp.transpose(wo[:, b * 128 : (b + 1) * 128])
        for i in range(4):
            blk = b * 4 + i
            wot[blk % 2, blk // 2] = part[i * 32 : (i + 1) * 32]
    for load in loads[:3] + loads[4:]:
        load.wait()

    pl.semaphore_wait(barrier, len(greeted))

    d2 = 2 - 4 * c

    def blk(a, zz):
        return g.at[a, c, x * 4 + zz]

    def to_x(a, zz):
        for d in (2, 1, 3):
            send(blk(a, zz), blk(a, zz), s_ab.at[a], r_b.at[a, d - 1], dev_x(d))

    def to_z(a):
        for v in (3, 2, 1):
            send(blk(a, z), blk(a, z), s_ab.at[a], r_a.at[a, v - 1], dev_z(zx(v)))

    def to_sib(a, d):
        chunk = g.at[a, c, pl.ds(((x - d + 4) % 4) * 4, 4)]
        send(chunk, chunk, s_c.at[a], r_c.at[a, d], sib)

    def put(a, half, d):
        xx = (x - d + 4) % 4
        rows = g[a, half, pl.ds(xx * 4, 4)].reshape(128, TOK)
        if a == T:
            lane = lax.broadcasted_iota(jnp.int32, (128, TOK), 1)
            rows = jnp.where(lane < count, rows.astype(F32), 0.0).astype(BF)
        col = pl.multiple_of(half * 512 + xx * 128, 128)
        xt[a, :, pl.ds(col, 128)] = jnp.transpose(rows)

    send(blk(M, z), blk(M, z), s_ab.at[M], r_a.at[M, 2], dev_ring(d2))
    send(blk(M, z), blk(M, z), s_ab.at[M], r_a.at[M, 0], dev_ring(1))
    send(blk(M, z), blk(M, z), s_ab.at[M], r_a.at[M, 1], dev_ring(-1))
    to_x(M, z)
    to_z(S)
    to_z(T)
    for d in range(1, 8):
        send(cs.at[y], cs.at[y], s_k.at[0], r_k.at[0], dev_y(d))
    for slot, zz in ((0, (z + 3) % 4), (1, (z + 1) % 4), (2, (z + 2) % 4)):
        wait(blk(M, zz), r_a.at[M, slot])
        to_x(M, zz)
    to_sib(M, 0)
    for a in (S, T):
        to_x(a, z)
        for v in (1, 2, 3):
            wait(blk(a, zx(v)), r_a.at[a, v - 1])
            to_x(a, zx(v))
        to_sib(a, 0)
        put(a - 1, c, 0)

    def arrive(a):
        for d in (1, 3, 2):
            wait(g.at[a, c, pl.ds(((x - d + 4) % 4) * 4, 4)], r_b.at[a, d - 1])
            to_sib(a, d)
            put(a, c, d)

    def arrive_sib(a):
        for d in (0, 1, 3, 2):
            wait(g.at[a, 1 - c, pl.ds(((x - d + 4) % 4) * 4, 4)], r_c.at[a, d])
            put(a, 1 - c, d)

    arrive(M)
    arrive_sib(M)
    k_s[...] = nn(xt[M], wk[...].reshape(1024, 512)).astype(BF)
    v_s[...] = nn(xt[M], wv[...].reshape(1024, 512)).astype(BF)
    kt_s[...] = jnp.transpose(k_s[...])
    vt_s[...] = jnp.transpose(v_s[...])
    arrive(S)
    arrive_sib(S)
    q_s[...] = nn(xt[S], wq[...].reshape(1024, 512)).astype(BF)

    def head(h):
        return slice(h * HEAD, (h + 1) * HEAD)

    for h in range(HEADS):
        scores = nt(k_s[:, head(h)], q_s[:, head(h)]) + bias[...]
        top = jnp.max(scores, axis=0, keepdims=True)
        e = jnp.exp(scores - top)
        probs = e * (1.0 / jnp.sum(e, axis=0, keepdims=True))
        low = probs.astype(BF)
        p_s[h] = probs
        pb_s[h] = low
        ot_s[head(h), :] = nn(vt_s[head(h), :], low).astype(BF)
        if h == 1:
            put(T, c, 0)
            arrive(T)

    orders = {
        OUT: [(zx(v), v - 1, dev_z(zx(v))) for v in (3, 2, 1)],
        GX: [(zx(v), v - 1, dev_z(zx(v))) for v in (3, 2, 1)],
        GM: [((z + 2) % 4, 2, dev_ring(-d2)), ((z + 1) % 4, 0, dev_ring(1)), ((z + 3) % 4, 1, dev_ring(-1))],
    }
    for i in orders:
        orders[i].append((z, 3, None))

    def sum_start(i, part):
        pb_out[i] = part(1 - c).astype(BF).reshape(4, 4, 32, TOK)
        for zz, key, _ in orders[i]:
            send(pb_out.at[i, :, zz], lc.at[i, :, zz], rs_c.at[i], rr_c.at[i, key], sib)
        po[i] = part(c).reshape(4, 4, 32, TOK)

    def sum_x(i):
        for zz, key, _ in orders[i]:
            wait(lc.at[i, :, zz], rr_c.at[i, key])
            total = po[i, :, zz] + lc[i, :, zz].astype(F32)
            po[i, :, zz] = total
            sx[i, :, zz] = total.astype(BF)
            for d in (2, 1, 3):
                send(sx.at[i, (x + d) % 4, zz], lx.at[i, zz, d - 1], rs_x.at[i], rr_x.at[i, key], dev_x(d))

    def sum_z(i):
        for zz, key, dev in orders[i]:
            wait(lx.at[i, zz], rr_x.at[i, key])
            got = lx[i, zz].astype(F32)
            total = po[i, x, zz] + got[0] + got[1] + got[2]
            if dev is None:
                uo[i] = total
            else:
                ub[i, zz] = total.astype(BF)
                send(ub.at[i, zz], lz.at[i, key], rs_z.at[i], rr_z.at[i, key], dev)

    def sum_end(i):
        for key in range(3):
            wait(lz.at[i, key], rr_z.at[i, key])
        got = lz[i].astype(F32)
        return uo[i] + got[0] + got[1] + got[2]

    sum_start(OUT, lambda half: nn(wot[half].reshape(512, 512), ot_s[...]))
    arrive_sib(T)
    do_s[...] = nn(xt[T], wot[...].reshape(1024, 512)).astype(BF)
    sum_x(OUT)

    inner_all = jnp.zeros((1, TOK), F32)
    for h in range(HEADS):
        dprob = nt(v_s[:, head(h)], do_s[:, head(h)])
        probs = p_s[h]
        inner = jnp.sum(probs * dprob, axis=0, keepdims=True)
        inner_all += inner
        ds = (probs * (dprob - inner)).astype(BF)
        dk_s[:, head(h)] = nn(ds, q_s[:, head(h)]).astype(BF)
        dv_s[:, head(h)] = nn(pb_s[h], do_s[:, head(h)]).astype(BF)
        dqt_s[head(h), :] = nn(kt_s[head(h), :], ds).astype(BF)

    def part_gm(half):
        return nt(wk[half].reshape(512, 512), dk_s[...]) + nt(wv[half].reshape(512, 512), dv_s[...])

    sum_start(GM, part_gm)
    sum_start(GX, lambda half: nn(wq[half].reshape(512, 512), dqt_s[...]))

    row = lax.broadcasted_iota(jnp.int32, (8, 128), 0)
    folded = jnp.broadcast_to(inner_all[:, :128] + inner_all[:, 128:], (8, 128))
    l0[c] = jnp.where(row == 0, folded, 0.0)
    send(l0.at[c], l0.at[c], s_l.at[0], r_l.at[0], sib)

    sum_z(OUT)
    sum_x(GM)
    wait(l0.at[1 - c], r_l.at[0])
    l1[x] = l0[0] + l0[1]
    for d in (1, 2, 3):
        send(l1.at[x], l1.at[x], s_l.at[1], r_l.at[1], dev_x(d))
    sum_x(GX)
    wait(l1.at[pl.ds(0, 3)], r_l.at[1])
    l2[z] = (l1[0] + l1[1]) + (l1[2] + l1[3])
    for v in (1, 2, 3):
        send(l2.at[z], l2.at[z], s_l.at[2], r_l.at[2], dev_z(zx(v)))
    sum_z(GM)
    wait(l2.at[pl.ds(0, 3)], r_l.at[2])
    l3[y] = (l2[0] + l2[1]) + (l2[2] + l2[3])
    for d in range(1, 8):
        send(l3.at[y], l3.at[y], s_l.at[3], r_l.at[3], dev_y(d))
    lp[p] = sum_end(GM).astype(BF)
    for d in (-4, 4):
        send(lp.at[p], lp.at[p], s_p.at[0], r_p.at[0], dev_ring(d))
    sum_z(GX)
    out_o[...] = sum_end(OUT).astype(BF)
    wait(cs.at[pl.ds(0, 7)], r_k.at[0])
    tot = jnp.sum(cs[...], axis=0)
    tot_row = tot[0:1, 0:1]
    tot_all = jnp.broadcast_to(tot_row, (32, TOK))
    wait(l3.at[pl.ds(0, 7)], r_l.at[3])
    loss = jnp.sum(jnp.sum(l3[...], axis=0), keepdims=True)
    loss_o[...] = jnp.broadcast_to(loss / tot_row, (8, 128))
    gx_o[...] = (sum_end(GX) / tot_all).astype(BF)
    wait(lp.at[pl.ds(0, 2)], r_p.at[0])
    got = lp[...].astype(F32)
    gm_o[...] = ((got[0] + got[1] + got[2]) / tot_all).astype(BF)

    for a in range(3):
        wait(g.at[a, 0, pl.ds(0, 15)], s_ab.at[a])
        wait(g.at[a, 0], s_c.at[a])
        wait(pb_out.at[a], rs_c.at[a])
        wait(sx.at[a, pl.ds(0, 3)], rs_x.at[a])
        wait(ub.at[a, pl.ds(0, 3)], rs_z.at[a])
    wait(lp.at[pl.ds(0, 2)], s_p.at[0])
    wait(cs.at[pl.ds(0, 7)], s_k.at[0])
    wait(l0.at[0], s_l.at[0])
    wait(l1.at[pl.ds(0, 3)], s_l.at[1])
    wait(l2.at[pl.ds(0, 3)], s_l.at[2])
    wait(l3.at[pl.ds(0, 7)], s_l.at[3])


def place_kernel(out_i, gx_i, gm_i, loss_i, out_o, gx_o, gm_o, loss_o):
    out_o[...] = out_i[...]
    gx_o[...] = gx_i[...]
    gm_o[...] = gm_i[...]
    loss_o[0] = loss_i[0, 0]


def local(memory, states, targets, w_query, w_key, w_value, w_out, src_ids, tgt_ids, counts):
    vmem = pl.BlockSpec(memory_space=pltpu.VMEM)
    smem = pl.BlockSpec(memory_space=pltpu.SMEM)
    hbm = pl.BlockSpec(memory_space=pl.ANY)
    dma = pltpu.SemaphoreType.DMA
    block = jax.ShapeDtypeStruct((32, TOK), BF)
    split = (16, 2, 32, 512)

    def v(shape, dtype=BF):
        return pltpu.VMEM(shape, dtype)

    results = pl.pallas_call(
        main_kernel,
        out_shape=(block, block, block, jax.ShapeDtypeStruct((8, 128), F32)),
        in_specs=[hbm] * 7 + [vmem, vmem, smem],
        out_specs=[vmem] * 4,
        scratch_shapes=[
            v((2, 16, 32, 512)), v((2, 16, 32, 512)), v((2, 16, 32, 512)), v((512, 1024)), v((2, 16, 32, 512)),
            v((3, 2, 16, 32, TOK)), v((3, TOK, 1024)), v((TOK, TOK), F32),
            v((TOK, 512)), v((TOK, 512)), v((TOK, 512)), v((512, TOK)), v((512, TOK)), v((TOK, 512)),
            v((HEADS, TOK, TOK), F32), v((HEADS, TOK, TOK)), v((512, TOK)), v((512, TOK)), v((TOK, 512)), v((TOK, 512)),
            v((3, 4, 4, 32, TOK)), v((3, 4, 4, 32, TOK), F32), v((3, 4, 4, 32, TOK)), v((3, 4, 4, 32, TOK)),
            v((3, 4, 3, 32, TOK)), v((3, 32, TOK), F32), v((3, 4, 32, TOK)), v((3, 3, 32, TOK)), v((3, 32, TOK)),
            v((8, 8, 128), F32), v((2, 8, 128), F32), v((4, 8, 128), F32), v((4, 8, 128), F32), v((8, 8, 128), F32),
            dma((10,)), dma((3, 3)), dma((3, 3)), dma((3, 4)), dma((3,)), dma((3,)),
            dma((3, 4)), dma((3, 4)), dma((3, 3)), dma((3,)), dma((3,)), dma((3,)),
            dma((1,)), dma((1,)), dma((1,)), dma((1,)), dma((4,)), dma((4,)),
        ],
        compiler_params=pltpu.CompilerParams(
            collective_id=0, has_side_effects=True, vmem_limit_bytes=50 * 1024 * 1024
        ),
        name="cross_attention",
    )(
        memory[0].T, states[0, 0].T, targets[0, 0].T,
        w_query.reshape(split), w_key.reshape(split), w_value.reshape(split), w_out[0],
        src_ids, tgt_ids, counts,
    )
    out, gx, gm, loss = pl.pallas_call(
        place_kernel,
        out_shape=(block, block, block, jax.ShapeDtypeStruct((1,), F32)),
        in_specs=[vmem] * 4,
        out_specs=[vmem, vmem, vmem, smem],
        name="place_outputs",
    )(*results)
    return out.T[None, None], loss, gx.T[None, None], gm.T[None]


def solution(mesh):
    placed = (
        P("dp", None, "mp"),
        P("phase", "dp", None, "mp"),
        P("phase", "dp", None, "mp"),
        P("phase", None, "mp"),
        P("phase", None, "mp"),
        P("phase", None, "mp"),
        P("phase", "mp", None),
        P("dp", None),
        P("dp", None),
        P("dp"),
    )
    return jax.shard_map(
        local,
        mesh=mesh,
        in_specs=placed,
        out_specs=(
            P("phase", "dp", None, "mp"),
            P("phase"),
            P("phase", "dp", None, "mp"),
            P("dp", None, "mp"),
        ),
        check_vma=False,
    )
```

time: 1120 us -> 67.2 us (0.06)
  the two profiles are of different devices: /device:TPU:8 before, /device:TPU:6 now
where the time goes in v1:
time: 67.2 us; the launch traced here: 66 us
  Pallas kernels  55.8 us (83%)
  local copies, waits for them, and re-layouts  8.89 us (13%)
  between operations  1.32 us (2%)
    pallas_call x1, Pallas kernels, local(): pl.pallas_call(main_kernel, out_shape=(block, block, block, jax.ShapeDtyp...  54.4 us
    unnamed x24, local copies, waits for them, and re-layouts  8.89 us
    pallas_call x1, Pallas kernels, local(): pl.pallas_call(place_kernel, out_shape=(block, block, block, jax.ShapeDty...  1.38 us

profile of v1, /device:TPU:6, one launch (start us, length us, event | category | flops | bytes accessed | tf_op | source)
XLA Modules:
  0.0 66.0 jit_solution(17127932712484061739)
XLA Ops:
  1.3 0.0 copy-start.11
  1.3 0.0 copy-start.10
  1.3 0.7 %copy-done.11 = s32[1,256]{1,0:T(1,128)S(1)} copy-done((s32[1,256]{1,0:T(1,128)S(1)}, s32[1,256]{1,0:T(1,128)}, u32[]{:S(2)}) %copy-start.11) | copy-done | bytes 1048
  2.0 0.0 copy-done.10
  2.0 0.0 copy-start
  2.0 1.2 %copy-done = bf16[1,1024,512]{2,1,0:T(8,128)(2,1)S(1)} copy-done((bf16[1,1024,512]{2,1,0:T(8,128)(2,1)S(1)}, bf16[1,1024,512]{2,1,0:T(8,128)(2,1)}, u32[]{:S(2)}) %copy-start) | copy-done | bytes 1048600
  3.2 0.0 copy-start.1
  3.2 1.2 %copy-done.1 = bf16[1,1024,512]{2,1,0:T(8,128)(2,1)S(1)} copy-done((bf16[1,1024,512]{2,1,0:T(8,128)(2,1)S(1)}, bf16[1,1024,512]{2,1,0:T(8,128)(2,1)}, u32[]{:S(2)}) %copy-start.1) | copy-done | bytes 1048600
  4.4 0.0 copy-start.2
  4.4 1.2 %copy-done.2 = bf16[1,1024,512]{2,1,0:T(8,128)(2,1)S(1)} copy-done((bf16[1,1024,512]{2,1,0:T(8,128)(2,1)S(1)}, bf16[1,1024,512]{2,1,0:T(8,128)(2,1)}, u32[]{:S(2)}) %copy-start.2) | copy-done | bytes 1048600
  5.7 0.0 copy-start.3
  5.7 0.7 %copy-done.3 = bf16[1,256,32]{1,2,0:T(8,128)(2,1)S(1)} copy-done((bf16[1,256,32]{1,2,0:T(8,128)(2,1)S(1)}, bf16[1,256,32]{1,2,0:T(8,128)(2,1)}, u32[]{:S(2)}) %copy-start.3) | copy-done | bytes 16408
  6.4 0.0 copy-start.4
  6.4 0.7 %copy-done.4 = bf16[1,1,256,32]{2,3,1,0:T(8,128)(2,1)S(1)} copy-done((bf16[1,1,256,32]{2,3,1,0:T(8,128)(2,1)S(1)}, bf16[1,1,256,32]{2,3,1,0:T(8,128)(2,1)}, u32[]{:S(2)}) %copy-start.4) | copy-done | bytes 16408
  7.1 0.0 copy-start.5
  7.1 0.7 %copy-done.5 = bf16[1,1,256,32]{2,3,1,0:T(8,128)(2,1)S(1)} copy-done((bf16[1,1,256,32]{2,3,1,0:T(8,128)(2,1)S(1)}, bf16[1,1,256,32]{2,3,1,0:T(8,128)(2,1)}, u32[]{:S(2)}) %copy-start.5) | copy-done | bytes 16408
  7.8 54.4 %cross_attention.1 = (bf16[32,256]{1,0:T(8,128)(2,1)S(1)}, bf16[32,256]{1,0:T(8,128)(2,1)S(1)}, bf16[32,256]{1,0:T(8,128)(2,1)S(1)}, f32[8,128]{1,0:T(8,128)S(1)}) custom-call(bf16[32,256]{1,0:T(8,128)(2,1)S(1)} %bitcast.25, bf16[32,256]{1,0:T(8,128)(2,1)S(1)} %bitcast.26, bf16[32,256]{1,0:T(8,128)(2,1)S(1)} %bitcast.27, ...), custom_call_target="tpu_custom_call" | custom-call | tf_op jit(solution)/shard_map/cross_attention/pallas_call | solution.py:313
  62.2 0.0 copy-start.6
  62.2 0.6 copy-done.6
  62.8 0.0 copy-start.7
  62.8 0.6 copy-done.7
  63.4 0.0 copy-start.8
  63.4 0.6 copy-done.8
  64.0 0.0 copy-start.9
  64.0 0.6 copy-done.9
  64.6 1.4 %place_outputs.1 = (bf16[32,256]{1,0:T(8,128)(2,1)}, bf16[32,256]{1,0:T(8,128)(2,1)}, bf16[32,256]{1,0:T(8,128)(2,1)}, f32[1]{0:T(128)}) custom-call(bf16[32,256]{1,0:T(8,128)(2,1)} %copy-done.6, bf16[32,256]{1,0:T(8,128)(2,1)} %copy-done.7, bf16[32,256]{1,0:T(8,128)(2,1)} %copy-done.8, f32[8,128]{1,0:T(8,128)} %copy-done.9), custom_call_target="tpu_custom_call" | custom-call | tf_op jit(solution)/shard_map/place_outputs/pallas_call | solution.py:339
Async XLA Ops:
  1.3 0.7 %copy-start.11 = (s32[1,256]{1,0:T(1,128)S(1)}, s32[1,256]{1,0:T(1,128)}, u32[]{:S(2)}) copy-start(s32[1,256]{1,0:T(1,128)} %tgt_ref.1) | copy-start | bytes 3076
  1.3 0.7 %copy-start.10 = (s32[1,256]{1,0:T(1,128)S(1)}, s32[1,256]{1,0:T(1,128)}, u32[]{:S(2)}) copy-start(s32[1,256]{1,0:T(1,128)} %src_ref.1) | copy-start | bytes 3076
  2.0 1.2 %copy-start = (bf16[1,1024,512]{2,1,0:T(8,128)(2,1)S(1)}, bf16[1,1024,512]{2,1,0:T(8,128)(2,1)}, u32[]{:S(2)}) copy-start(bf16[1,1024,512]{2,1,0:T(8,128)(2,1)} %param.13) | copy-start | bytes 3145732
  3.2 1.2 %copy-start.1 = (bf16[1,1024,512]{2,1,0:T(8,128)(2,1)S(1)}, bf16[1,1024,512]{2,1,0:T(8,128)(2,1)}, u32[]{:S(2)}) copy-start(bf16[1,1024,512]{2,1,0:T(8,128)(2,1)} %param.14) | copy-start | bytes 3145732
  4.4 1.2 %copy-start.2 = (bf16[1,1024,512]{2,1,0:T(8,128)(2,1)S(1)}, bf16[1,1024,512]{2,1,0:T(8,128)(2,1)}, u32[]{:S(2)}) copy-start(bf16[1,1024,512]{2,1,0:T(8,128)(2,1)} %param.15) | copy-start | bytes 3145732
  5.7 0.7 %copy-start.3 = (bf16[1,256,32]{1,2,0:T(8,128)(2,1)S(1)}, bf16[1,256,32]{1,2,0:T(8,128)(2,1)}, u32[]{:S(2)}) copy-start(bf16[1,256,32]{1,2,0:T(8,128)(2,1)} %param.10) | copy-start | bytes 49156
  6.4 0.7 %copy-start.4 = (bf16[1,1,256,32]{2,3,1,0:T(8,128)(2,1)S(1)}, bf16[1,1,256,32]{2,3,1,0:T(8,128)(2,1)}, u32[]{:S(2)}) copy-start(bf16[1,1,256,32]{2,3,1,0:T(8,128)(2,1)} %param.11) | copy-start | bytes 49156
  7.1 0.7 %copy-start.5 = (bf16[1,1,256,32]{2,3,1,0:T(8,128)(2,1)S(1)}, bf16[1,1,256,32]{2,3,1,0:T(8,128)(2,1)}, u32[]{:S(2)}) copy-start(bf16[1,1,256,32]{2,3,1,0:T(8,128)(2,1)} %param.12) | copy-start | bytes 49156
  62.2 0.6 copy-start.6
  62.8 0.6 copy-start.7
  63.4 0.6 copy-start.8
  64.0 0.6 copy-start.9

commit v2 on v1

--- a/solution.py
+++ b/solution.py
@@ -26,10 +26,10 @@
 
 
 def main_kernel(
-    mem_in, st_in, tg_in, wq_in, wk_in, wv_in, wo_in, src_ref, tgt_ref, cnt_ref,
+    mem_in, st_in, tg_in, wq_in, wk_in, wv_in, wo_in, src_in, tgt_in, cnt_ref,
     out_o, gx_o, gm_o, loss_o,
-    wq, wk, wv, wo, wot, g, xt, bias,
-    q_s, k_s, v_s, kt_s, vt_s, do_s, p_s, pb_s, ot_s, dqt_s, dk_s, dv_s,
+    wq, wk, wv, wo, wot, g, xt, bias, src_ref, tgt_ref,
+    q_s, k_s, v_s, kt_s, vt_s, do_s, p_s, pb_s, ds_s, ot_s, dqt_s, dk_s, dv_s,
     pb_out, po, lc, sx, lx, uo, ub, lz, lp, cs, l0, l1, l2, l3,
     lw, r_a, r_b, r_c, s_ab, s_c, rr_c, rr_x, rr_z, rs_c, rs_x, rs_z, r_p, s_p, r_k, s_k, r_l, s_l,
 ):
@@ -71,7 +71,8 @@
     for i, (src, dst) in enumerate(((wk_in, wk), (wv_in, wv), (wq_in, wq))):
         for h in range(2):
             loads.append(pltpu.make_async_copy(src.at[:, h], dst.at[h], lw.at[4 + 2 * i + h]))
-    for load in loads:
+    ids = [pltpu.make_async_copy(src, dst, lw.at[10 + i]) for i, (src, dst) in enumerate(((src_in, src_ref), (tgt_in, tgt_ref)))]
+    for load in loads + ids:
         load.start()
 
     barrier = pltpu.get_barrier_semaphore()
@@ -81,18 +82,9 @@
         pl.semaphore_signal(barrier, inc=1, device_id=dev, device_id_type=MESH)
 
     count = cnt_ref[0]
-    src_col = jnp.transpose(jnp.broadcast_to(src_ref[...].astype(F32), (TOK, TOK)))
-    bias[...] = jnp.where(src_col == tgt_ref[...].astype(F32), 0.0, NEG)
     cs[y] = jnp.full((8, 128), count.astype(F32))
-    loads[3].wait()
-    for b in range(8):
-        part = jnp.transpose(wo[:, b * 128 : (b + 1) * 128])
-        for i in range(4):
-            blk = b * 4 + i
-            wot[blk % 2, blk // 2] = part[i * 32 : (i + 1) * 32]
-    for load in loads[:3] + loads[4:]:
+    for load in loads[:3]:
         load.wait()
-
     pl.semaphore_wait(barrier, len(greeted))
 
     d2 = 2 - 4 * c
@@ -129,6 +121,18 @@
     to_z(T)
     for d in range(1, 8):
         send(cs.at[y], cs.at[y], s_k.at[0], r_k.at[0], dev_y(d))
+
+    for load in ids:
+        load.wait()
+    src_col = jnp.transpose(jnp.broadcast_to(src_ref[...].astype(F32), (TOK, TOK)))
+    bias[...] = jnp.where(src_col == tgt_ref[...].astype(F32), 0.0, NEG)
+    loads[3].wait()
+    for b in range(8):
+        part = jnp.transpose(wo[:, b * 128 : (b + 1) * 128])
+        for i in range(4):
+            at = b * 4 + i
+            wot[at % 2, at // 2] = part[i * 32 : (i + 1) * 32]
+
     for slot, zz in ((0, (z + 3) % 4), (1, (z + 1) % 4), (2, (z + 2) % 4)):
         wait(blk(M, zz), r_a.at[M, slot])
         to_x(M, zz)
@@ -154,6 +158,8 @@
 
     arrive(M)
     arrive_sib(M)
+    for load in loads[4:]:
+        load.wait()
     k_s[...] = nn(xt[M], wk[...].reshape(1024, 512)).astype(BF)
     v_s[...] = nn(xt[M], wv[...].reshape(1024, 512)).astype(BF)
     kt_s[...] = jnp.transpose(k_s[...])
@@ -178,39 +184,45 @@
             put(T, c, 0)
             arrive(T)
 
-    orders = {
-        OUT: [(zx(v), v - 1, dev_z(zx(v))) for v in (3, 2, 1)],
-        GX: [(zx(v), v - 1, dev_z(zx(v))) for v in (3, 2, 1)],
-        GM: [((z + 2) % 4, 2, dev_ring(-d2)), ((z + 1) % 4, 0, dev_ring(1)), ((z + 3) % 4, 1, dev_ring(-1))],
-    }
-    for i in orders:
-        orders[i].append((z, 3, None))
+    along_z = [(zx(v), v - 1, dev_z(zx(v))) for v in (3, 2, 1)] + [(z, 3, None)]
+    along_ring = [((z + 2) % 4, 2, dev_ring(-d2)), ((z + 1) % 4, 0, dev_ring(1)), ((z + 3) % 4, 1, dev_ring(-1))]
+    along_x = [((x + d) % 4, d - 1, dev_x(d)) for d in (2, 1, 3)] + [(x, 3, None)]
+
+    def chunk(i, buf, at):
+        return buf.at[i, at] if i == GM else buf.at[i, :, at]
 
     def sum_start(i, part):
         pb_out[i] = part(1 - c).astype(BF).reshape(4, 4, 32, TOK)
-        for zz, key, _ in orders[i]:
-            send(pb_out.at[i, :, zz], lc.at[i, :, zz], rs_c.at[i], rr_c.at[i, key], sib)
+        for at, key, _ in along_x if i == GM else along_z:
+            send(chunk(i, pb_out, at), chunk(i, lc, at), rs_c.at[i], rr_c.at[i, key], sib)
         po[i] = part(c).reshape(4, 4, 32, TOK)
 
-    def sum_x(i):
-        for zz, key, _ in orders[i]:
-            wait(lc.at[i, :, zz], rr_c.at[i, key])
-            total = po[i, :, zz] + lc[i, :, zz].astype(F32)
-            po[i, :, zz] = total
-            sx[i, :, zz] = total.astype(BF)
-            for d in (2, 1, 3):
-                send(sx.at[i, (x + d) % 4, zz], lx.at[i, zz, d - 1], rs_x.at[i], rr_x.at[i, key], dev_x(d))
-
-    def sum_z(i):
-        for zz, key, dev in orders[i]:
-            wait(lx.at[i, zz], rr_x.at[i, key])
-            got = lx[i, zz].astype(F32)
-            total = po[i, x, zz] + got[0] + got[1] + got[2]
+    def sum_first(i):
+        for at, key, _ in along_x if i == GM else along_z:
+            wait(chunk(i, lc, at), rr_c.at[i, key])
+            if i == GM:
+                total = po[i, at] + lc[i, at].astype(F32)
+                po[i, at] = total
+                sx[i, at] = total.astype(BF)
+                for zz, slot, dev in along_ring:
+                    send(sx.at[i, at, zz], lx.at[i, at, slot], rs_x.at[i], rr_x.at[i, key], dev)
+            else:
+                total = po[i, :, at] + lc[i, :, at].astype(F32)
+                po[i, :, at] = total
+                sx[i, :, at] = total.astype(BF)
+                for xx, slot, dev in along_x[:3]:
+                    send(sx.at[i, xx, at], lx.at[i, at, slot], rs_x.at[i], rr_x.at[i, key], dev)
+
+    def sum_second(i):
+        for at, key, dev in along_x if i == GM else along_z:
+            wait(lx.at[i, at], rr_x.at[i, key])
+            got = lx[i, at].astype(F32)
+            total = (po[i, at, z] if i == GM else po[i, x, at]) + got[0] + got[1] + got[2]
             if dev is None:
                 uo[i] = total
             else:
-                ub[i, zz] = total.astype(BF)
-                send(ub.at[i, zz], lz.at[i, key], rs_z.at[i], rr_z.at[i, key], dev)
+                ub[i, at] = total.astype(BF)
+                send(ub.at[i, at], lz.at[i, key], rs_z.at[i], rr_z.at[i, key], dev)
 
     def sum_end(i):
         for key in range(3):
@@ -221,7 +233,7 @@
     sum_start(OUT, lambda half: nn(wot[half].reshape(512, 512), ot_s[...]))
     arrive_sib(T)
     do_s[...] = nn(xt[T], wot[...].reshape(1024, 512)).astype(BF)
-    sum_x(OUT)
+    sum_first(OUT)
 
     inner_all = jnp.zeros((1, TOK), F32)
     for h in range(HEADS):
@@ -229,7 +241,14 @@
         probs = p_s[h]
         inner = jnp.sum(probs * dprob, axis=0, keepdims=True)
         inner_all += inner
-        ds = (probs * (dprob - inner)).astype(BF)
+        ds_s[h] = (probs * (dprob - inner)).astype(BF)
+    row = lax.broadcasted_iota(jnp.int32, (8, 128), 0)
+    folded = jnp.broadcast_to(inner_all[:, :128] + inner_all[:, 128:], (8, 128))
+    l3[y] = jnp.where(row == 0, folded, 0.0)
+    for d in range(1, 8):
+        send(l3.at[y], l3.at[y], s_l.at[3], r_l.at[3], dev_y(d))
+    for h in range(HEADS):
+        ds = ds_s[h]
         dk_s[:, head(h)] = nn(ds, q_s[:, head(h)]).astype(BF)
         dv_s[:, head(h)] = nn(pb_s[h], do_s[:, head(h)]).astype(BF)
         dqt_s[head(h), :] = nn(kt_s[head(h), :], ds).astype(BF)
@@ -240,38 +259,32 @@
     sum_start(GM, part_gm)
     sum_start(GX, lambda half: nn(wq[half].reshape(512, 512), dqt_s[...]))
 
-    row = lax.broadcasted_iota(jnp.int32, (8, 128), 0)
-    folded = jnp.broadcast_to(inner_all[:, :128] + inner_all[:, 128:], (8, 128))
-    l0[c] = jnp.where(row == 0, folded, 0.0)
+    sum_first(GM)
+    sum_first(GX)
+    sum_second(OUT)
+    wait(l3.at[pl.ds(0, 7)], r_l.at[3])
+    l0[c] = jnp.sum(l3[...], axis=0)
     send(l0.at[c], l0.at[c], s_l.at[0], r_l.at[0], sib)
-
-    sum_z(OUT)
-    sum_x(GM)
+    sum_second(GM)
     wait(l0.at[1 - c], r_l.at[0])
     l1[x] = l0[0] + l0[1]
     for d in (1, 2, 3):
         send(l1.at[x], l1.at[x], s_l.at[1], r_l.at[1], dev_x(d))
-    sum_x(GX)
+    lp[p] = sum_end(GM).astype(BF)
+    for d in (-4, 4):
+        send(lp.at[p], lp.at[p], s_p.at[0], r_p.at[0], dev_ring(d))
     wait(l1.at[pl.ds(0, 3)], r_l.at[1])
     l2[z] = (l1[0] + l1[1]) + (l1[2] + l1[3])
     for v in (1, 2, 3):
         send(l2.at[z], l2.at[z], s_l.at[2], r_l.at[2], dev_z(zx(v)))
-    sum_z(GM)
-    wait(l2.at[pl.ds(0, 3)], r_l.at[2])
-    l3[y] = (l2[0] + l2[1]) + (l2[2] + l2[3])
-    for d in range(1, 8):
-        send(l3.at[y], l3.at[y], s_l.at[3], r_l.at[3], dev_y(d))
-    lp[p] = sum_end(GM).astype(BF)
-    for d in (-4, 4):
-        send(lp.at[p], lp.at[p], s_p.at[0], r_p.at[0], dev_ring(d))
-    sum_z(GX)
+    sum_second(GX)
     out_o[...] = sum_end(OUT).astype(BF)
     wait(cs.at[pl.ds(0, 7)], r_k.at[0])
     tot = jnp.sum(cs[...], axis=0)
     tot_row = tot[0:1, 0:1]
     tot_all = jnp.broadcast_to(tot_row, (32, TOK))
-    wait(l3.at[pl.ds(0, 7)], r_l.at[3])
-    loss = jnp.sum(jnp.sum(l3[...], axis=0), keepdims=True)
+    wait(l2.at[pl.ds(0, 3)], r_l.at[2])
+    loss = jnp.sum((l2[0] + l2[1]) + (l2[2] + l2[3]), keepdims=True)
     loss_o[...] = jnp.broadcast_to(loss / tot_row, (8, 128))
     gx_o[...] = (sum_end(GX) / tot_all).astype(BF)
     wait(lp.at[pl.ds(0, 2)], r_p.at[0])
@@ -313,22 +326,23 @@
     results = pl.pallas_call(
         main_kernel,
         out_shape=(block, block, block, jax.ShapeDtypeStruct((8, 128), F32)),
-        in_specs=[hbm] * 7 + [vmem, vmem, smem],
+        in_specs=[hbm] * 9 + [smem],
         out_specs=[vmem] * 4,
         scratch_shapes=[
             v((2, 16, 32, 512)), v((2, 16, 32, 512)), v((2, 16, 32, 512)), v((512, 1024)), v((2, 16, 32, 512)),
             v((3, 2, 16, 32, TOK)), v((3, TOK, 1024)), v((TOK, TOK), F32),
+            v((1, TOK), jnp.int32), v((1, TOK), jnp.int32),
             v((TOK, 512)), v((TOK, 512)), v((TOK, 512)), v((512, TOK)), v((512, TOK)), v((TOK, 512)),
-            v((HEADS, TOK, TOK), F32), v((HEADS, TOK, TOK)), v((512, TOK)), v((512, TOK)), v((TOK, 512)), v((TOK, 512)),
+            v((HEADS, TOK, TOK), F32), v((HEADS, TOK, TOK)), v((HEADS, TOK, TOK)), v((512, TOK)), v((512, TOK)), v((TOK, 512)), v((TOK, 512)),
             v((3, 4, 4, 32, TOK)), v((3, 4, 4, 32, TOK), F32), v((3, 4, 4, 32, TOK)), v((3, 4, 4, 32, TOK)),
             v((3, 4, 3, 32, TOK)), v((3, 32, TOK), F32), v((3, 4, 32, TOK)), v((3, 3, 32, TOK)), v((3, 32, TOK)),
             v((8, 8, 128), F32), v((2, 8, 128), F32), v((4, 8, 128), F32), v((4, 8, 128), F32), v((8, 8, 128), F32),
-            dma((10,)), dma((3, 3)), dma((3, 3)), dma((3, 4)), dma((3,)), dma((3,)),
+            dma((12,)), dma((3, 3)), dma((3, 3)), dma((3, 4)), dma((3,)), dma((3,)),
             dma((3, 4)), dma((3, 4)), dma((3, 3)), dma((3,)), dma((3,)), dma((3,)),
             dma((1,)), dma((1,)), dma((1,)), dma((1,)), dma((4,)), dma((4,)),
         ],
         compiler_params=pltpu.CompilerParams(
-            collective_id=0, has_side_effects=True, vmem_limit_bytes=50 * 1024 * 1024
+            collective_id=0, has_side_effects=True, vmem_limit_bytes=62 * 1024 * 1024
         ),
         name="cross_attention",
     )(
@@ -339,7 +353,7 @@
     out, gx, gm, loss = pl.pallas_call(
         place_kernel,
         out_shape=(block, block, block, jax.ShapeDtypeStruct((1,), F32)),
-        in_specs=[vmem] * 4,
+        in_specs=[vmem, vmem, vmem, smem],
         out_specs=[vmem, vmem, vmem, smem],
         name="place_outputs",
     )(*results)

time: 67.2 us -> 55 us (0.82); the launches traced: 66 us -> 54.7 us
  local copies, waits for them, and re-layouts: 8.89 us -> 0 us
  Pallas kernels: 55.8 us -> 53.4 us
    unnamed x24 -> x0, local copies, waits for them, and re-layouts: 8.89 us -> none
    pallas_call x1, Pallas kernels: 54.4 us -> 51.9 us  [local(): pl.pallas_call(main_kernel, out_shape=(block, block, block, jax.ShapeDtyp...]
where the time goes in v2:
time: 55 us; the launch traced here: 54.7 us
  Pallas kernels  53.4 us (97%)
  between operations  1.29 us (2%)
    pallas_call x1, Pallas kernels, local(): pl.pallas_call(main_kernel, out_shape=(block, block, block, jax.ShapeDtyp...  51.9 us
    pallas_call x1, Pallas kernels, local(): pl.pallas_call(place_kernel, out_shape=(block, block, block, jax.ShapeDty...  1.49 us

profile of v2, /device:TPU:6, one launch (start us, length us, event | category | flops | bytes accessed | tf_op | source)
XLA Modules:
  0.0 54.7 jit_solution(12693011096188945403)
XLA Ops:
  1.3 51.9 %cross_attention.1 = (bf16[32,256]{1,0:T(8,128)(2,1)}, bf16[32,256]{1,0:T(8,128)(2,1)}, bf16[32,256]{1,0:T(8,128)(2,1)}, f32[8,128]{1,0:T(8,128)}) custom-call(bf16[32,256]{1,0:T(8,128)(2,1)} %bitcast.26, bf16[32,256]{1,0:T(8,128)(2,1)} %bitcast.27, bf16[32,256]{1,0:T(8,128)(2,1)} %bitcast.28, bf16[16,2,32,512]{3,2,1,0:T(8,128)(2,1)} %bitcast.22, ...), custom_call_target="tpu_custom_call" | custom-call | tf_op jit(solution)/shard_map/cross_attention/pallas_call | solution.py:326
  53.2 1.5 %place_outputs.1 = (bf16[32,256]{1,0:T(8,128)(2,1)}, bf16[32,256]{1,0:T(8,128)(2,1)}, bf16[32,256]{1,0:T(8,128)(2,1)}, f32[1]{0:T(128)}) custom-call(bf16[32,256]{1,0:T(8,128)(2,1)} %get-tuple-element.12.out_i, bf16[32,256]{1,0:T(8,128)(2,1)} %get-tuple-element.13.gx_i, bf16[32,256]{1,0:T(8,128)(2,1)} %get-tuple-element.14.gm_i, ...), custom_call_target="tpu_custom_call" | custom-call | tf_op jit(solution)/shard_map/place_outputs/pallas_call | solution.py:353

commit v3 on v2

--- a/solution.py
+++ b/solution.py
@@ -65,8 +65,7 @@
     def wait(ref, sem):
         pltpu.make_async_copy(ref, ref, sem).wait()
 
-    own = x * 4 + z
-    loads = [pltpu.make_async_copy(src, g.at[a, c, own], lw.at[a]) for a, src in ((M, mem_in), (S, st_in), (T, tg_in))]
+    loads = [pltpu.make_async_copy(src, g.at[a, c, x, z], lw.at[a]) for a, src in ((M, mem_in), (S, st_in), (T, tg_in))]
     loads.append(pltpu.make_async_copy(wo_in, wo, lw.at[3]))
     for i, (src, dst) in enumerate(((wk_in, wk), (wv_in, wv), (wq_in, wq))):
         for h in range(2):
@@ -90,7 +89,7 @@
     d2 = 2 - 4 * c
 
     def blk(a, zz):
-        return g.at[a, c, x * 4 + zz]
+        return g.at[a, c, x, zz]
 
     def to_x(a, zz):
         for d in (2, 1, 3):
@@ -101,23 +100,33 @@
             send(blk(a, z), blk(a, z), s_ab.at[a], r_a.at[a, v - 1], dev_z(zx(v)))
 
     def to_sib(a, d):
-        chunk = g.at[a, c, pl.ds(((x - d + 4) % 4) * 4, 4)]
-        send(chunk, chunk, s_c.at[a], r_c.at[a, d], sib)
+        part = g.at[a, c, (x - d + 4) % 4]
+        send(part, part, s_c.at[a], r_c.at[a, d], sib)
 
     def put(a, half, d):
         xx = (x - d + 4) % 4
-        rows = g[a, half, pl.ds(xx * 4, 4)].reshape(128, TOK)
+        rows = g[a, half, xx].reshape(128, TOK)
         if a == T:
             lane = lax.broadcasted_iota(jnp.int32, (128, TOK), 1)
             rows = jnp.where(lane < count, rows.astype(F32), 0.0).astype(BF)
         col = pl.multiple_of(half * 512 + xx * 128, 128)
         xt[a, :, pl.ds(col, 128)] = jnp.transpose(rows)
 
-    send(blk(M, z), blk(M, z), s_ab.at[M], r_a.at[M, 2], dev_ring(d2))
-    send(blk(M, z), blk(M, z), s_ab.at[M], r_a.at[M, 0], dev_ring(1))
-    send(blk(M, z), blk(M, z), s_ab.at[M], r_a.at[M, 1], dev_ring(-1))
+    rings = ((2, (z + 2) % 4, dev_ring(d2)), (0, (z + 3) % 4, dev_ring(1)), (1, (z + 1) % 4, dev_ring(-1)))
+
+    def to_ring(xx):
+        part = g.at[M, c, xx, z]
+        for slot, _, dev in rings:
+            send(part, part, s_ab.at[M], r_a.at[M, slot], dev)
+
+    def to_sib_m(key, zz):
+        part = g.at[M, c, :, zz]
+        send(part, part, s_c.at[M], r_c.at[M, key], sib)
+
     to_x(M, z)
     to_z(S)
+    to_ring(x)
+    to_x(S, z)
     to_z(T)
     for d in range(1, 8):
         send(cs.at[y], cs.at[y], s_k.at[0], r_k.at[0], dev_y(d))
@@ -133,40 +142,52 @@
             at = b * 4 + i
             wot[at % 2, at // 2] = part[i * 32 : (i + 1) * 32]
 
-    for slot, zz in ((0, (z + 3) % 4), (1, (z + 1) % 4), (2, (z + 2) % 4)):
-        wait(blk(M, zz), r_a.at[M, slot])
-        to_x(M, zz)
-    to_sib(M, 0)
+    for d in (1, 3, 2):
+        xx = (x - d + 4) % 4
+        wait(g.at[M, c, xx, z], r_b.at[M, d - 1])
+        to_ring(xx)
+    to_sib_m(3, z)
     for a in (S, T):
-        to_x(a, z)
+        if a == T:
+            to_x(a, z)
         for v in (1, 2, 3):
             wait(blk(a, zx(v)), r_a.at[a, v - 1])
             to_x(a, zx(v))
         to_sib(a, 0)
-        put(a - 1, c, 0)
+    put(S, c, 0)
+
+    def arrive_m():
+        for slot, zz, _ in (rings[1], rings[2], rings[0]):
+            wait(g.at[M, c, :, zz], r_a.at[M, slot])
+            to_sib_m(slot, zz)
+        for d in range(4):
+            put(M, c, d)
+        for key, zz in ((3, z), (0, (z + 3) % 4), (1, (z + 1) % 4), (2, (z + 2) % 4)):
+            wait(g.at[M, 1 - c, :, zz], r_c.at[M, key])
+        for d in range(4):
+            put(M, 1 - c, d)
 
     def arrive(a):
         for d in (1, 3, 2):
-            wait(g.at[a, c, pl.ds(((x - d + 4) % 4) * 4, 4)], r_b.at[a, d - 1])
+            wait(g.at[a, c, (x - d + 4) % 4], r_b.at[a, d - 1])
             to_sib(a, d)
             put(a, c, d)
 
     def arrive_sib(a):
         for d in (0, 1, 3, 2):
-            wait(g.at[a, 1 - c, pl.ds(((x - d + 4) % 4) * 4, 4)], r_c.at[a, d])
+            wait(g.at[a, 1 - c, (x - d + 4) % 4], r_c.at[a, d])
             put(a, 1 - c, d)
 
-    arrive(M)
-    arrive_sib(M)
     for load in loads[4:]:
         load.wait()
+    arrive(S)
+    arrive_sib(S)
+    q_s[...] = nn(xt[S], wq[...].reshape(1024, 512)).astype(BF)
+    arrive_m()
     k_s[...] = nn(xt[M], wk[...].reshape(1024, 512)).astype(BF)
     v_s[...] = nn(xt[M], wv[...].reshape(1024, 512)).astype(BF)
     kt_s[...] = jnp.transpose(k_s[...])
     vt_s[...] = jnp.transpose(v_s[...])
-    arrive(S)
-    arrive_sib(S)
-    q_s[...] = nn(xt[S], wq[...].reshape(1024, 512)).astype(BF)
 
     def head(h):
         return slice(h * HEAD, (h + 1) * HEAD)
@@ -248,18 +269,17 @@
     for d in range(1, 8):
         send(l3.at[y], l3.at[y], s_l.at[3], r_l.at[3], dev_y(d))
     for h in range(HEADS):
-        ds = ds_s[h]
-        dk_s[:, head(h)] = nn(ds, q_s[:, head(h)]).astype(BF)
+        dk_s[:, head(h)] = nn(ds_s[h], q_s[:, head(h)]).astype(BF)
         dv_s[:, head(h)] = nn(pb_s[h], do_s[:, head(h)]).astype(BF)
-        dqt_s[head(h), :] = nn(kt_s[head(h), :], ds).astype(BF)
 
     def part_gm(half):
         return nt(wk[half].reshape(512, 512), dk_s[...]) + nt(wv[half].reshape(512, 512), dv_s[...])
 
     sum_start(GM, part_gm)
+    for h in range(HEADS):
+        dqt_s[head(h), :] = nn(kt_s[head(h), :], ds_s[h]).astype(BF)
+    sum_first(GM)
     sum_start(GX, lambda half: nn(wq[half].reshape(512, 512), dqt_s[...]))
-
-    sum_first(GM)
     sum_first(GX)
     sum_second(OUT)
     wait(l3.at[pl.ds(0, 7)], r_l.at[3])
@@ -292,7 +312,7 @@
     gm_o[...] = ((got[0] + got[1] + got[2]) / tot_all).astype(BF)
 
     for a in range(3):
-        wait(g.at[a, 0, pl.ds(0, 15)], s_ab.at[a])
+        wait(k_s.at[pl.ds(0, 240)], s_ab.at[a])
         wait(g.at[a, 0], s_c.at[a])
         wait(pb_out.at[a], rs_c.at[a])
         wait(sx.at[a, pl.ds(0, 3)], rs_x.at[a])
@@ -330,7 +350,7 @@
         out_specs=[vmem] * 4,
         scratch_shapes=[
             v((2, 16, 32, 512)), v((2, 16, 32, 512)), v((2, 16, 32, 512)), v((512, 1024)), v((2, 16, 32, 512)),
-            v((3, 2, 16, 32, TOK)), v((3, TOK, 1024)), v((TOK, TOK), F32),
+            v((3, 2, 4, 4, 32, TOK)), v((3, TOK, 1024)), v((TOK, TOK), F32),
             v((1, TOK), jnp.int32), v((1, TOK), jnp.int32),
             v((TOK, 512)), v((TOK, 512)), v((TOK, 512)), v((512, TOK)), v((512, TOK)), v((TOK, 512)),
             v((HEADS, TOK, TOK), F32), v((HEADS, TOK, TOK)), v((HEADS, TOK, TOK)), v((512, TOK)), v((512, TOK)), v((TOK, 512)), v((TOK, 512)),

time: 55 us -> 53.3 us (0.969); the launches traced: 54.7 us -> 52.3 us
  Pallas kernels: 53.4 us -> 51 us
    pallas_call x1, Pallas kernels: 51.9 us -> 49.5 us  [local(): pl.pallas_call(main_kernel, out_shape=(block, block, block, jax.ShapeDtyp...]
where the time goes in v3:
time: 53.3 us; the launch traced here: 52.3 us
  Pallas kernels  51 us (96%)
  between operations  1.29 us (2%)
    pallas_call x1, Pallas kernels, local(): pl.pallas_call(main_kernel, out_shape=(block, block, block, jax.ShapeDtyp...  49.5 us
    pallas_call x1, Pallas kernels, local(): pl.pallas_call(place_kernel, out_shape=(block, block, block, jax.ShapeDty...  1.49 us

profile of v3, /device:TPU:6, one launch (start us, length us, event | category | flops | bytes accessed | tf_op | source)
XLA Modules:
  0.0 52.3 jit_solution(12963542498792561260)
XLA Ops:
  1.3 49.5 %cross_attention.1 = (bf16[32,256]{1,0:T(8,128)(2,1)}, bf16[32,256]{1,0:T(8,128)(2,1)}, bf16[32,256]{1,0:T(8,128)(2,1)}, f32[8,128]{1,0:T(8,128)}) custom-call(bf16[32,256]{1,0:T(8,128)(2,1)} %bitcast.26, bf16[32,256]{1,0:T(8,128)(2,1)} %bitcast.27, bf16[32,256]{1,0:T(8,128)(2,1)} %bitcast.28, bf16[16,2,32,512]{3,2,1,0:T(8,128)(2,1)} %bitcast.22, ...), custom_call_target="tpu_custom_call" | custom-call | tf_op jit(solution)/shard_map/cross_attention/pallas_call | solution.py:346
  50.8 1.5 %place_outputs.1 = (bf16[32,256]{1,0:T(8,128)(2,1)}, bf16[32,256]{1,0:T(8,128)(2,1)}, bf16[32,256]{1,0:T(8,128)(2,1)}, f32[1]{0:T(128)}) custom-call(bf16[32,256]{1,0:T(8,128)(2,1)} %get-tuple-element.12.out_i, bf16[32,256]{1,0:T(8,128)(2,1)} %get-tuple-element.13.gx_i, bf16[32,256]{1,0:T(8,128)(2,1)} %get-tuple-element.14.gm_i, ...), custom_call_target="tpu_custom_call" | custom-call | tf_op jit(solution)/shard_map/place_outputs/pallas_call | solution.py:373

commit v4 on v3

--- a/solution.py
+++ b/solution.py
@@ -186,6 +186,8 @@
     arrive_m()
     k_s[...] = nn(xt[M], wk[...].reshape(1024, 512)).astype(BF)
     v_s[...] = nn(xt[M], wv[...].reshape(1024, 512)).astype(BF)
+    put(T, c, 0)
+    arrive(T)
     kt_s[...] = jnp.transpose(k_s[...])
     vt_s[...] = jnp.transpose(v_s[...])
 
@@ -201,9 +203,6 @@
         p_s[h] = probs
         pb_s[h] = low
         ot_s[head(h), :] = nn(vt_s[head(h), :], low).astype(BF)
-        if h == 1:
-            put(T, c, 0)
-            arrive(T)
 
     along_z = [(zx(v), v - 1, dev_z(zx(v))) for v in (3, 2, 1)] + [(z, 3, None)]
     along_ring = [((z + 2) % 4, 2, dev_ring(-d2)), ((z + 1) % 4, 0, dev_ring(1)), ((z + 3) % 4, 1, dev_ring(-1))]

time: 53.3 us -> 53.2 us (level)
  no operation moved by 1% of the time
where the time goes in v4:
time: 53.2 us; the launch traced here: 52.2 us
  Pallas kernels  51 us (96%)
  between operations  1.29 us (2%)
    pallas_call x1, Pallas kernels, local(): pl.pallas_call(main_kernel, out_shape=(block, block, block, jax.ShapeDtyp...  49.5 us
    pallas_call x1, Pallas kernels, local(): pl.pallas_call(place_kernel, out_shape=(block, block, block, jax.ShapeDty...  1.49 us

profile of v4, /device:TPU:6, one launch (start us, length us, event | category | flops | bytes accessed | tf_op | source)
XLA Modules:
  0.0 52.2 jit_solution(7289766263897117952)
XLA Ops:
  1.3 49.5 %cross_attention.1 = (bf16[32,256]{1,0:T(8,128)(2,1)}, bf16[32,256]{1,0:T(8,128)(2,1)}, bf16[32,256]{1,0:T(8,128)(2,1)}, f32[8,128]{1,0:T(8,128)}) custom-call(bf16[32,256]{1,0:T(8,128)(2,1)} %bitcast.26, bf16[32,256]{1,0:T(8,128)(2,1)} %bitcast.27, bf16[32,256]{1,0:T(8,128)(2,1)} %bitcast.28, bf16[16,2,32,512]{3,2,1,0:T(8,128)(2,1)} %bitcast.22, ...), custom_call_target="tpu_custom_call" | custom-call | tf_op jit(solution)/shard_map/cross_attention/pallas_call | solution.py:345
  50.8 1.5 %place_outputs.1 = (bf16[32,256]{1,0:T(8,128)(2,1)}, bf16[32,256]{1,0:T(8,128)(2,1)}, bf16[32,256]{1,0:T(8,128)(2,1)}, f32[1]{0:T(128)}) custom-call(bf16[32,256]{1,0:T(8,128)(2,1)} %get-tuple-element.12.out_i, bf16[32,256]{1,0:T(8,128)(2,1)} %get-tuple-element.13.gx_i, bf16[32,256]{1,0:T(8,128)(2,1)} %get-tuple-element.14.gm_i, ...), custom_call_target="tpu_custom_call" | custom-call | tf_op jit(solution)/shard_map/place_outputs/pallas_call | solution.py:372
